TPU v7x, 32 devices: a whole 2x2x4 slice. The times are simulated.
32 devices in a mesh: dp: 8 (over z, y), tensor: 4 (over x, core).
Axes of the slice: x: 2, y: 2, z: 4, core: 2. Of those that a mesh axis runs over, the one named last changes fastest.
Arguments:
- queries: bfloat16 [4096, 4096], P('dp', 'tensor'), may hold values from -6 to 6
- passages: bfloat16 [2048, 4096], P('dp', 'tensor'), may hold values from -6 to 6
- neg_lists: int32 [64, 16], replicated, may hold values from -1 to 127, as said below
- positives: int32 [4096], P('dp'), may hold values from 0 to 2047, as said below
Outputs:
- query_grad: bfloat16 [4096, 4096], P('dp', 'tensor')
- passage_grad: bfloat16 [2048, 4096], P('dp', 'tensor')
- query_loss: float32 [4096], P('dp')
Inputs may be any that keep to these rules, and one draw needn't show every extreme that they name: `neg_lists`: each row names distinct blocks, its live entries first and then -1, with 8 or more live. The rows of query blocks d * 8 to (d + 1) * 8 - 1 name at most 64 distinct blocks, and at most 8 distinct blocks of one owner, blocks d * 16 to (d + 1) * 16 - 1 belonging to index d of dp. `positives`: the positive of a query is a passage of a live block in its query block's row.
All inputs are finite; a program needn't handle non-finite values.
Results may differ from a plain program's by a relative error of at most 0.0051.
Values may be sent and summed in bfloat16 or wider, within the bound.
A program may use at most 128 MiB of HBM per device.

v0:
```python
from functools import partial

import jax
import jax.numpy as jnp
from jax import lax
from jax.sharding import PartitionSpec as P

MINP = 64
NPRE = 7
PBLK = 16


EPS = 1e-06
INV_TEMP = 20.0


def prefix(value, axis, join, neutral, backward):
    count, mine = (lax.axis_size(axis), lax.axis_index(axis))
    pieces = jax.tree.map(lambda part: lax.all_gather(part, axis), value)
    if backward:
        pieces = jax.tree.map(lambda part: part[::-1], pieces)
        mine = count - 1 - mine
    subtotal = jax.tree.map(
        lambda part, zero: jnp.full_like(part, 0) + jnp.asarray(zero, part.dtype), value, neutral
    )

    def step(position, subtotal):
        longer = join(subtotal, jax.tree.map(lambda part: part[position], pieces))
        return jax.tree.map(lambda new, old: jnp.where(position < mine, new, old), longer, subtotal)

    return lax.fori_loop(0, count - 1, step, subtotal)


def prefix_terms(dot_sums, query_sq, passage_sq, cand_mask, labels, weight):
    query_scale = lax.rsqrt(query_sq + EPS)
    passage_scale = jnp.where(cand_mask, lax.rsqrt(passage_sq + EPS), 0.0)
    logits = dot_sums * query_scale[..., :, None] * passage_scale[..., None, :] * INV_TEMP
    exponent = jnp.where(cand_mask[..., None, :], jnp.exp(logits), 0.0)
    exp_total = jnp.sum(exponent, axis=-1)
    probability = exponent / exp_total[..., None]
    cross_entropy = jnp.log(exp_total) - jnp.sum(labels * logits, axis=-1)
    gradient = weight * (probability - labels)
    coefficient = gradient * query_scale[..., :, None] * passage_scale[..., None, :] * INV_TEMP
    inner_term = gradient * logits
    row_term = jnp.square(query_scale) * jnp.sum(inner_term, axis=-1)
    col_term = jnp.square(passage_scale) * jnp.sum(inner_term, axis=-2)
    return (coefficient, row_term, col_term, weight * cross_entropy)


def add_parts(earlier, later):
    return tuple((earlier_part + later_part for earlier_part, later_part in zip(earlier, later)))


def shard_plan(shard_number, shard_width, prefix_sizes):
    low_col = shard_number * shard_width
    owned_ends = [
        prefix_size - low_col
        for prefix_size in prefix_sizes
        if low_col < prefix_size <= low_col + shard_width
    ]
    cut_points = sorted(set([0, shard_width] + owned_ends))
    return (list(zip(cut_points[:-1], cut_points[1:])), owned_ends)


def request_plan(flat_ids, capacity, per_owner):
    entry_count = flat_ids.shape[0]
    is_valid = flat_ids >= 0
    entry_order = jnp.arange(entry_count, dtype=jnp.int32)
    earlier = entry_order[None, :] < entry_order[:, None]
    same_block = (flat_ids[:, None] == flat_ids[None, :]) & is_valid[None, :]
    is_first = is_valid & jnp.logical_not(jnp.any(same_block & earlier, axis=1))
    owner_index = jnp.where(is_valid, flat_ids // per_owner, 0)
    local_block = jnp.where(is_valid, flat_ids % per_owner, 0)
    owner_rank = jnp.sum(
        ((owner_index[:, None] == owner_index[None, :]) & earlier & is_first[None, :]).astype(
            jnp.int32
        ),
        axis=1,
    )
    home_slot = jnp.where(is_first, owner_index * capacity + owner_rank, 0)
    entry_slot = jnp.sum(jnp.where(same_block & is_first[None, :], home_slot[None, :], 0), axis=1)
    return (is_first, home_slot, entry_slot, local_block)


def per_device(queries, passages, neg_lists, positives):
    peer_count = lax.axis_size("dp")
    shards = lax.axis_size("tensor")
    shard_width = queries.shape[1]
    blocks_here = neg_lists.shape[0] // peer_count
    neg_count = neg_lists.shape[1]
    block_rows = queries.shape[0] // blocks_here
    local_blocks = passages.shape[0] // PBLK
    capacity = blocks_here * neg_count // 2 // peer_count
    slot_count = peer_count * capacity
    cand_count = neg_count * PBLK
    my_index = lax.axis_index("dp")
    shard_index = lax.axis_index("tensor")
    query_mat = queries.reshape(blocks_here, block_rows, shard_width)
    passage_mat = passages.reshape(local_blocks, PBLK, shard_width)
    flat_all = neg_lists.reshape(peer_count, blocks_here * neg_count)
    is_first, home_slot, entry_slot, local_block = jax.vmap(
        partial(request_plan, capacity=capacity, per_owner=local_blocks)
    )(flat_all)
    targets = my_index * capacity + jnp.arange(capacity, dtype=jnp.int32)
    target_hit = is_first[:, :, None] & (home_slot[:, :, None] == targets[None, None, :])
    wanted = (
        jnp.sum(jnp.where(target_hit, local_block[:, :, None] + 1, 0), axis=1).reshape(slot_count)
        - 1
    )
    is_live = wanted >= 0
    panels = jnp.where(
        is_live[:, None, None], passage_mat[jnp.maximum(wanted, 0)], jnp.zeros((), jnp.bfloat16)
    )
    fetched = lax.all_to_all(panels, "dp", split_axis=0, concat_axis=0, tiled=True)
    own_ids = lax.dynamic_index_in_dim(flat_all, my_index, 0, keepdims=False)
    own_slot = lax.dynamic_index_in_dim(entry_slot, my_index, 0, keepdims=False)
    own_valid = own_ids >= 0
    candidates = jnp.where(own_valid[:, None, None], fetched[own_slot], jnp.zeros((), jnp.bfloat16))
    candidates = candidates.reshape(blocks_here, cand_count, shard_width)
    cand_mask = jnp.repeat(own_valid.reshape(blocks_here, neg_count), PBLK, axis=1)
    cand_ids = (
        jnp.where(own_valid, own_ids, 0)[:, None] * PBLK
        + jnp.arange(PBLK, dtype=jnp.int32)[None, :]
    ).reshape(blocks_here, cand_count)
    positive_rows = positives.reshape(blocks_here, block_rows)
    labels = ((cand_ids[:, None, :] == positive_rows[:, :, None]) & cand_mask[:, None, :]).astype(
        jnp.float32
    )
    prefix_sizes = [MINP * 2**level_index for level_index in range(NPRE)]
    weight_total = sum((prefix_size / MINP for prefix_size in prefix_sizes))
    shard_plans = [
        shard_plan(shard_number, shard_width, prefix_sizes) for shard_number in range(shards)
    ]
    most_owned = max(1, max((len(plan_item[1]) for plan_item in shard_plans)))
    tile_shape = (blocks_here, block_rows, cand_count)

    def forward_branch(shard_number):
        segments, owned_ends = shard_plans[shard_number]

        def forward_branch_body(operand):
            dot_sums = jnp.zeros(tile_shape, jnp.float32)
            query_sq = jnp.zeros((blocks_here, block_rows), jnp.float32)
            passage_sq = jnp.zeros((blocks_here, cand_count), jnp.float32)
            kept_sums = []
            for low_col, high_col in segments:
                query_seg = query_mat[:, :, low_col:high_col]
                passage_seg = candidates[:, :, low_col:high_col]
                dot_sums = dot_sums + jnp.einsum(
                    "bqw,bcw->bqc", query_seg, passage_seg, preferred_element_type=jnp.float32
                )
                query_sq = query_sq + jnp.sum(jnp.square(query_seg.astype(jnp.float32)), axis=-1)
                passage_sq = passage_sq + jnp.sum(
                    jnp.square(passage_seg.astype(jnp.float32)), axis=-1
                )
                if high_col in owned_ends:
                    kept_sums.append((dot_sums, query_sq, passage_sq))
            for filler in range(most_owned - len(kept_sums)):
                kept_sums.append(
                    (jnp.zeros_like(dot_sums), jnp.zeros_like(query_sq), jnp.zeros_like(passage_sq))
                )
            stacked = tuple(
                (jnp.stack([kept_item[member] for kept_item in kept_sums]) for member in range(3))
            )
            return ((dot_sums, query_sq, passage_sq), stacked)

        return forward_branch_body

    full_sums, kept_stack = lax.switch(
        shard_index, [forward_branch(shard_number) for shard_number in range(shards)], 0
    )
    earlier_sums = prefix(
        (full_sums[0], full_sums[1], full_sums[2]),
        "tensor",
        add_parts,
        (jnp.zeros_like(full_sums[0]), jnp.zeros_like(full_sums[1]), jnp.zeros_like(full_sums[2])),
        False,
    )

    def middle_branch(shard_number):
        segments, owned_ends = shard_plans[shard_number]

        def middle_branch_body(operand):
            coef_sum = jnp.zeros(tile_shape, jnp.float32)
            row_sum = jnp.zeros((blocks_here, block_rows), jnp.float32)
            col_sum = jnp.zeros((blocks_here, cand_count), jnp.float32)
            loss_sum = jnp.zeros((blocks_here, block_rows), jnp.float32)
            coef_list, row_list, col_list = ([], [], [])
            for rank_owned, end_col in enumerate(owned_ends):
                prefix_size = shard_number * shard_width + end_col
                coefficient, row_term, col_term, weighted = prefix_terms(
                    earlier_sums[0] + kept_stack[0][rank_owned],
                    earlier_sums[1] + kept_stack[1][rank_owned],
                    earlier_sums[2] + kept_stack[2][rank_owned],
                    cand_mask,
                    labels,
                    prefix_size / MINP,
                )
                coef_sum = coef_sum + coefficient
                row_sum = row_sum + row_term
                col_sum = col_sum + col_term
                loss_sum = loss_sum + weighted
                coef_list.append(coefficient)
                row_list.append(row_term)
                col_list.append(col_term)
            for filler in range(most_owned - len(coef_list)):
                coef_list.append(jnp.zeros_like(coef_sum))
                row_list.append(jnp.zeros_like(row_sum))
                col_list.append(jnp.zeros_like(col_sum))
            stacked = (jnp.stack(coef_list), jnp.stack(row_list), jnp.stack(col_list))
            return ((coef_sum, row_sum, col_sum), loss_sum, stacked)

        return middle_branch_body

    own_sums, loss_sum, term_stack = lax.switch(
        shard_index, [middle_branch(shard_number) for shard_number in range(shards)], 0
    )
    query_loss = lax.psum(loss_sum, "tensor") / weight_total
    later_sums = prefix(
        (own_sums[0], own_sums[1], own_sums[2]),
        "tensor",
        add_parts,
        (jnp.zeros_like(own_sums[0]), jnp.zeros_like(own_sums[1]), jnp.zeros_like(own_sums[2])),
        True,
    )

    def backward_branch(shard_number):
        segments, owned_ends = shard_plans[shard_number]

        def backward_branch_body(operand):
            sum_coef, sum_row, sum_col = later_sums
            query_parts, passage_parts = ([], [])
            for low_col, high_col in reversed(segments):
                if high_col in owned_ends:
                    rank_owned = owned_ends.index(high_col)
                    sum_coef = sum_coef + term_stack[0][rank_owned]
                    sum_row = sum_row + term_stack[1][rank_owned]
                    sum_col = sum_col + term_stack[2][rank_owned]
                coef_half = sum_coef.astype(jnp.bfloat16)
                query_seg = query_mat[:, :, low_col:high_col]
                passage_seg = candidates[:, :, low_col:high_col]
                query_parts.append(
                    jnp.einsum(
                        "bqc,bcw->bqw", coef_half, passage_seg, preferred_element_type=jnp.float32
                    )
                    - sum_row[..., None] * query_seg.astype(jnp.float32)
                )
                passage_parts.append(
                    jnp.einsum(
                        "bqc,bqw->bcw", coef_half, query_seg, preferred_element_type=jnp.float32
                    )
                    - sum_col[..., None] * passage_seg.astype(jnp.float32)
                )
            query_grad = jnp.concatenate(query_parts[::-1], axis=-1).astype(jnp.bfloat16)
            cand_grad = jnp.concatenate(passage_parts[::-1], axis=-1)
            return (query_grad, cand_grad)

        return backward_branch_body

    query_grad, cand_grad = lax.switch(
        shard_index, [backward_branch(shard_number) for shard_number in range(shards)], 0
    )
    cand_grad = cand_grad.reshape(blocks_here * neg_count, PBLK, shard_width)
    cand_grad = jnp.where(own_valid[:, None, None], cand_grad, 0.0)
    slot_grad = jnp.zeros((slot_count, PBLK, shard_width), jnp.float32).at[own_slot].add(cand_grad)
    returned = lax.all_to_all(slot_grad, "dp", split_axis=0, concat_axis=0, tiled=True)
    target_rows = jnp.where(is_live, wanted, local_blocks)
    passage_grad = (
        jnp.zeros((local_blocks, PBLK, shard_width), jnp.float32)
        .at[target_rows]
        .add(returned, mode="drop")
    )
    return (
        query_grad.reshape(blocks_here * block_rows, shard_width),
        passage_grad.reshape(local_blocks * PBLK, shard_width).astype(jnp.bfloat16),
        query_loss.reshape(blocks_here * block_rows),
    )


def solution(mesh):
    return jax.shard_map(
        per_device,
        mesh=mesh,
        in_specs=(P("dp", "tensor"), P("dp", "tensor"), P(), P("dp")),
        out_specs=(P("dp", "tensor"), P("dp", "tensor"), P("dp")),
        check_vma=False,
    )
```

profile of v0, /device:TPU:0, one launch (start us, length us, event | category | flops | bytes accessed | tf_op | source)
XLA Modules:
  0.0 327.5 jit_solution(18100214042088260628)
XLA Ops:
  11.5 3.2 broadcast_select_fusion.1
  14.6 7.3 %all-to-all-start = ((bf16[64,16,1024]{2,1,0:T(8,128)(2,1)}), bf16[64,16,1024]{2,1,0:T(8,128)(2,1)S(1)}, u32[]{:S(2)}, u32[]{:S(2)}) async-start(bf16[64,16,1024]{2,1,0:T(8,128)(2,1)} %broadcast_select_fusion.1), calls=%async_computation | async-start | bytes 4194304 | tf_op jit(solution)/shard_map/all_to_all | solution.py:114
  22.7 47.5 %all-to-all-done = bf16[64,16,1024]{2,1,0:T(8,128)(2,1)S(1)} async-done(((bf16[64,16,1024]{2,1,0:T(8,128)(2,1)}), bf16[64,16,1024]{2,1,0:T(8,128)(2,1)S(1)}, u32[]{:S(2)}, u32[]{:S(2)}) %all-to-all-start) | async-done | bytes 2097184 | tf_op jit(solution)/shard_map/all_to_all | solution.py:114
  70.1 2.7 gather_fusion.1
  72.9 3.9 %bitcast_select_fusion = bf16[8,256,1024]{2,1,0:T(8,128)(2,1)} fusion(pred[8,256]{1,0:T(8,128)(4,1)S(1)} %broadcast_in_dim.218, bf16[8,256,1024]{2,1,0:T(8,128)(2,1)} %bitcast.436), kind=kLoop, calls=%fused_computation.304 | loop fusion | flops 2097152 | bytes 8390656 | tf_op jit(solution)/shard_map/jit(_where)/select_n | solution.py:118
  76.8 20.4 %conditional.3 = (f32[8,64,256]{2,1,0:T(8,128)}, f32[8,64]{1,0:T(8,128)}, f32[8,256]{1,0:T(8,128)}, f32[5,8,64,256]{3,2,1,0:T(8,128)}, f32[5,8,64]{2,1,0:T(8,128)S(1)}, /*index=5*/f32[5,8,256]{2,1,0:T(8,128)S(1)}) conditional(s32[]{:T(128)} %clamp.2, (bf16[8,64,1024]{2,1,0:T(8,128)(2,1)S(1)}, ...), branch_computations={%region_4.15_spmd, %region_15.18_spmd, %region_18.21_spmd, %region... | conditional | flops 276839424 | bytes 43454540 | solution.py:168
  76.8 6.4 %copy.64 = bf16[8,256,1024]{1,2,0:T(8,128)(2,1)} copy(bf16[8,256,1024]{2,1,0:T(8,128)(2,1)} %get-tuple-element.600) | data formatting | bytes 8388608 | tf_op jit(solution)/shard_map
  87.4 2.1 bitcast_dynamic-update-slice_fusion.2
  97.8 5.4 %all-gather.1 = f32[32,64]{1,0:T(8,128)S(1)} all-gather(f32[8,64]{1,0:T(8,128)} %get-tuple-element.496), channel_id=3, replica_groups=mesh['dp'=8,'tensor'=4] {'tensor'}, dimensions={0}, use_global_device_ids=true | all-gather | bytes 10240 | tf_op jit(solution)/shard_map/all_gather | solution.py:19
  103.2 5.5 %all-gather.2 = f32[32,256]{1,0:T(8,128)S(1)} all-gather(f32[8,256]{1,0:T(8,128)} %get-tuple-element.497), channel_id=4, replica_groups=mesh['dp'=8,'tensor'=4] {'tensor'}, dimensions={0}, use_global_device_ids=true | all-gather | bytes 40960 | tf_op jit(solution)/shard_map/all_gather | solution.py:19
  108.7 9.5 %all-gather.9.cloned.1.call-done = f32[32,64,256]{2,1,0:T(8,128)} async-done(((f32[8,64,256]{2,1,0:T(8,128)}), f32[32,64,256]{2,1,0:T(8,128)}) %all-gather.9.cloned.1.call-update) | async-done | bytes 2097168 | tf_op jit(solution)/shard_map/all_gather | solution.py:19
  118.3 3.9 %while.36 = (s32[]{:T(128)}, f32[8,64,256]{2,1,0:T(8,128)S(1)}, f32[8,64]{1,0:T(8,128)S(1)}, f32[8,256]{1,0:T(8,128)S(1)}, s32[]{:T(128)}, /*index=5*/f32[4,8,64...) while((s32[]{:T(128)}, f32[8,64,256]{2,1,0:T(8,128)S(1)}, ...), condition=%wide.region_25.26_spmd.clone, body=%wide.region_24.25_spmd.clone.sunk | while | flops 400900 | bytes 1603729 | solution.py:31
  122.1 12.9 %conditional.4 = (f32[8,64,256]{2,1,0:T(8,128)}, f32[8,64]{1,0:T(8,128)}, f32[8,256]{1,0:T(8,128)}, f32[8,64]{1,0:T(8,128)S(1)}, f32[5,8,64,256]{3,2,1,0:T(8,128...) conditional(s32[]{:T(128)} %clamp.2, (pred[8,16,16]{2,1,0:T(8,128)(4,1)S(1)}, ...), branch_computations={%region_26.47_spmd, %region_47.52_spmd, %region_52.53_spmd, %regio... | conditional | flops 18176000 | bytes 21162040 | solution.py:214
  122.3 2.6 fusion.34
  135.1 5.4 %all-gather.4 = f32[32,64]{1,0:T(8,128)S(1)} all-gather(f32[8,64]{1,0:T(8,128)} %get-tuple-element.505), channel_id=6, replica_groups=mesh['dp'=8,'tensor'=4] {'tensor'}, dimensions={0}, use_global_device_ids=true | all-gather | bytes 10240 | tf_op jit(solution)/shard_map/all_gather | solution.py:19
  140.5 5.4 %all-gather.5 = f32[32,256]{1,0:T(8,128)S(1)} all-gather(f32[8,256]{1,0:T(8,128)} %get-tuple-element.506), channel_id=7, replica_groups=mesh['dp'=8,'tensor'=4] {'tensor'}, dimensions={0}, use_global_device_ids=true | all-gather | bytes 40960 | tf_op jit(solution)/shard_map/all_gather | solution.py:19
  145.9 11.8 %all-gather.11.cloned.1.call-done = f32[32,64,256]{2,1,0:T(8,128)} async-done(((f32[8,64,256]{2,1,0:T(8,128)}), f32[32,64,256]{2,1,0:T(8,128)}) %all-gather.11.cloned.1.call-update) | async-done | bytes 2097168 | tf_op jit(solution)/shard_map/all_gather | solution.py:19
  157.8 3.2 rev.9
  160.9 3.9 %while.37 = (s32[]{:T(128)}, f32[8,64,256]{2,1,0:T(8,128)S(1)}, f32[8,64]{1,0:T(8,128)S(1)}, f32[8,256]{1,0:T(8,128)S(1)}, s32[]{:T(128)}, /*index=5*/f32[4,8,64...) while((s32[]{:T(128)}, f32[8,64,256]{2,1,0:T(8,128)S(1)}, ...), condition=%wide.region_59.60_spmd.clone, body=%wide.region_58.59_spmd.clone.sunk | while | flops 400900 | bytes 1603729 | solution.py:31
  164.8 40.9 %conditional.5 = (bf16[512,1024]{1,0:T(8,128)(2,1)}, f32[128,16,1024]{2,1,0:T(8,128)}) conditional(s32[]{:T(128)} %clamp.2, (f32[5,8,64,256]{3,2,1,0:T(8,128)}, f32[8,64,256]{2,1,0:T(8,128)S(1)}, bf16[8,256,1024]{2,1,0:T(8,128)(2,1)}, f32[5,8,64]{2,1,0:T(8,128)S(1)}, f32[8,64]{1,0:T(8,128)S(1)}, ...), branch_computations={%region_60.61_spmd, %region_61.62_spmd, %region_62.63_spmd, %regio... | conditional | flops 546845184 | bytes 96241816 | solution.py:259
  168.2 6.5 %copy.65 = bf16[8,256,1024]{1,2,0:T(8,128)(2,1)} copy(bf16[8,256,1024]{2,1,0:T(8,128)(2,1)} %get-tuple-element.603) | data formatting | bytes 8388608 | tf_op jit(solution)/shard_map
  186.9 2.8 convolution_subtract_fusion
  189.7 3.1 multiply_subtract_fusion.1
  192.8 2.7 multiply_subtract_fusion
  195.5 10.1 %concatenate.17 = f32[8,256,1024]{2,1,0:T(8,128)} concatenate(f32[8,256,64]{2,1,0:T(8,128)S(1)} %copy.61, f32[8,256,64]{2,1,0:T(8,128)S(1)} %copy-done.12, f32[8,256,128]{2,1,0:T(8,128)} %convolution_subtract_fusion, f32[8,256,256]{2,1,0:T(8,128)} %multiply_subtract_fusion.1, f32[8,256,512]{2,1,0:T(8,128)} %multiply_subtract_fusion), dimensions={2} | concatenate | bytes 16777216 | tf_op jit(solution)/shard_map/cond/branch_0_fun/concatenate | solution.py:254
  205.7 7.2 %broadcast_select_fusion = f32[128,16,1024]{2,1,0:T(8,128)} fusion(f32[128,16,1024]{2,1,0:T(8,128)} %get-tuple-element.513, pred[128]{0:T(512)(128)(4,1)S(1)} %compare_bitcast_fusion), kind=kLoop, calls=%fused_computation.305 | loop fusion | flops 2097152 | bytes 16777344 | tf_op jit(solution)/shard_map/jit(_where)/select_n | solution.py:263
  212.9 2.5 broadcast_in_dim.228
  215.3 26.6 %scatter_fusion = f32[64,16,1024]{2,1,0:T(8,128)} fusion(f32[64,16,1024]{2,1,0:T(8,128)} %broadcast_in_dim.228, s32[128]{0:T(128)S(1)} %fusion.127, f32[128,16,1024]{2,1,0:T(8,128)} %broadcast_select_fusion), kind=kCustom, calls=%fused_computation.2 | custom fusion | flops 2097152 | bytes 25166336 | tf_op jit(solution)/shard_map/scatter-add | solution.py:264
  241.9 5.5 %all-to-all-start.1 = ((f32[64,16,1024]{2,1,0:T(8,128)}), f32[64,16,1024]{2,1,0:T(8,128)}, u32[]{:S(2)}, u32[]{:S(2)}) async-start(f32[64,16,1024]{2,1,0:T(8,128)} %scatter_fusion), calls=%async_computation.1 | async-start | bytes 8388608 | tf_op jit(solution)/shard_map/all_to_all | solution.py:265
  247.4 6.1 %psum.7 = f32[8,64]{1,0:T(8,128)S(1)} all-reduce(f32[8,64]{1,0:T(8,128)S(1)} %get-tuple-element.514), channel_id=1, replica_groups=mesh['dp'=8,'tensor'=4] {'tensor'}, use_global_device_ids=true, to_apply=%region_66.67 | all-reduce | flops 512 | bytes 4096 | tf_op jit(solution)/shard_map/psum | solution.py:217
  254.1 56.7 %all-to-all-done.1 = f32[64,16,1024]{2,1,0:T(8,128)} async-done(((f32[64,16,1024]{2,1,0:T(8,128)}), f32[64,16,1024]{2,1,0:T(8,128)}, u32[]{:S(2)}, u32[]{:S(2)}) %all-to-all-start.1) | async-done | bytes 4194336 | tf_op jit(solution)/shard_map/all_to_all | solution.py:265
  311.0 8.8 %scatter_fusion.1 = f32[16,16,1024]{2,1,0:T(8,128)S(1)} fusion(f32[16,16,1024]{2,1,0:T(8,128)S(1)} %broadcast_in_dim.227, s32[64]{0:T(128)S(1)} %get-tuple-element.754, f32[64,16,1024]{2,1,0:T(8,128)} %all-to-all-done.1), kind=kCustom, calls=%fused_computation.3 | custom fusion | flops 1048576 | bytes 12583168 | tf_op jit(solution)/shard_map/scatter-add | solution.py:270
  (149 shorter events, 51.6 us)
Async XLA Ops:
  7.2 2.3 copy-start
  14.6 55.5 %all-to-all-start = ((bf16[64,16,1024]{2,1,0:T(8,128)(2,1)}), bf16[64,16,1024]{2,1,0:T(8,128)(2,1)S(1)}, u32[]{:S(2)}, u32[]{:S(2)}) async-start(bf16[64,16,1024]{2,1,0:T(8,128)(2,1)} %broadcast_select_fusion.1), calls=%async_computation | async-start | bytes 4194304 | tf_op jit(solution)/shard_map/all_to_all | solution.py:114
  21.9 96.4 %all-gather.9.cloned.1.call-start = ((), (), s32[]{:S(2)}) async-start(), calls=%async_computation.2 | async-start | bytes 2621440 | tf_op jit(solution)/shard_map/all_gather | solution.py:19
  72.9 3.9 %copy-start.11 = (bf16[512,1024]{1,0:T(8,128)(2,1)S(1)}, bf16[512,1024]{1,0:T(8,128)(2,1)}, u32[]{:S(2)}) copy-start(bf16[512,1024]{1,0:T(8,128)(2,1)} %param.20) | copy-start | bytes 3145732
  76.8 20.5 %copy-start.15 = (s32[512]{0:T(512)S(1)}, s32[512]{0:T(512)}, u32[]{:S(2)}) copy-start(s32[512]{0:T(512)} %param.23) | copy-start | bytes 6148
  83.2 6.3 %copy-start.2 = (bf16[8,256,1024]{2,1,0:T(8,128)(2,1)S(1)}, bf16[8,256,1024]{2,1,0:T(8,128)(2,1)}, u32[]{:S(2)}) copy-start(bf16[8,256,1024]{2,1,0:T(8,128)(2,1)} %get-tuple-element.600) | copy-start | bytes 12582916 | tf_op jit(solution)/shard_map/cond
  97.2 60.5 %all-gather.11.cloned.1.call-start = ((), (), s32[]{:S(2)}) async-start(), calls=%async_computation.3 | async-start | bytes 2621440 | tf_op jit(solution)/shard_map/all_gather | solution.py:19
  166.6 10.7 %copy-start.13 = (bf16[8,64,256]{2,1,0:T(8,128)(2,1)}, bf16[8,64,256]{2,1,0:T(8,128)(2,1)S(1)}, u32[]{:S(2)}) copy-start(bf16[8,64,256]{2,1,0:T(8,128)(2,1)S(1)} %get-tuple-element.713) | copy-start | bytes 786436 | tf_op jit(solution)/shard_map/cond
  168.2 7.9 %copy-start.14 = (bf16[8,64,256]{2,1,0:T(8,128)(2,1)}, bf16[8,64,256]{2,1,0:T(8,128)(2,1)S(1)}, u32[]{:S(2)}) copy-start(bf16[8,64,256]{2,1,0:T(8,128)(2,1)S(1)} %get-tuple-element.721) | copy-start | bytes 786436 | tf_op jit(solution)/shard_map/cond
  174.8 5.3 %copy-start.6 = (bf16[8,256,1024]{2,1,0:T(8,128)(2,1)S(1)}, bf16[8,256,1024]{2,1,0:T(8,128)(2,1)}, u32[]{:S(2)}) copy-start(bf16[8,256,1024]{2,1,0:T(8,128)(2,1)} %get-tuple-element.603) | copy-start | bytes 12582916 | tf_op jit(solution)/shard_map/cond
  186.9 5.9 %copy-start.7 = (bf16[8,256,1024]{2,1,0:T(8,128)(2,1)S(1)}, bf16[8,256,1024]{2,1,0:T(8,128)(2,1)}, u32[]{:S(2)}) copy-start(bf16[8,256,1024]{2,1,0:T(8,128)(2,1)} %get-tuple-element.603) | copy-start | bytes 12582916 | tf_op jit(solution)/shard_map/cond
  192.8 2.8 copy-start.12
  241.9 69.0 %all-to-all-start.1 = ((f32[64,16,1024]{2,1,0:T(8,128)}), f32[64,16,1024]{2,1,0:T(8,128)}, u32[]{:S(2)}, u32[]{:S(2)}) async-start(f32[64,16,1024]{2,1,0:T(8,128)} %scatter_fusion), calls=%async_computation.1 | async-start | bytes 8388608 | tf_op jit(solution)/shard_map/all_to_all | solution.py:265
  310.9 9.8 %copy-start.1 = (bf16[256,1024]{1,0:T(8,128)(2,1)S(1)}, bf16[256,1024]{1,0:T(8,128)(2,1)}, u32[]{:S(2)}) copy-start(bf16[256,1024]{1,0:T(8,128)(2,1)} %param.21) | copy-start | bytes 1572868
Sparse Core Ops, SparseCore 0:
  97.3 20.8 all-gather.8
  135.2 22.5 all-gather.10
where the time goes:
time: 329 us; the launch traced here: 328 us
  waiting for transfers between devices  126 us (38%)
  other arithmetic  79.9 us (24%)
  local copies, waits for them, and re-layouts  39.8 us (12%)
  blocking collectives  27.8 us (8%)
  matrix products  26.3 us (8%)
  between operations  14.3 us (4%)
  starting transfers between devices  12.9 us (4%)
    all_to_all x1, waiting for transfers between devices, per_device(): lax.all_to_all(slot_grad, 'dp', split_axis=0, concat_axis=0, tiled=True)  56.7 us
    all_to_all x1, waiting for transfers between devices, per_device(): lax.all_to_all(panels, 'dp', split_axis=0, concat_axis=0, tiled=True)  47.5 us
    scatter-add x1, other arithmetic, per_device(): jnp.zeros((slot_count, PBLK, shard_width), jnp.float32).at[own_slot]  26.6 us
    all_gather x4, blocking collectives, prefix(): pieces = jax.tree.map(lambda part: lax.all_gather(part, axis), value)  21.7 us
    all_gather x2, waiting for transfers between devices, prefix(): pieces = jax.tree.map(lambda part: lax.all_gather(part, axis), value)  21.4 us
    another operation x2, local copies, waits for them, and re-layouts  13 us
    dot_general x5, matrix products, backward_branch_body(): jnp.einsum('bqc,bqw->bcw', coef_half, query_seg, preferred_element_type=j...  11.2 us
    concatenate x1, local copies, waits for them, and re-layouts, backward_branch_body(): cand_grad = jnp.concatenate(passage_parts[::-1], axis=-1)  10.1 us
  transfers between devices with their start and end apart: 4, of which 4 were waited for; matrix products, arithmetic and copies ran while one was open for 1% of the time, Pallas kernels for 0%

commit v1 on v0

v1 whole, which is shorter than its diff:
```python
from functools import partial

import jax
import jax.numpy as jnp
from jax import lax
from jax.experimental import pallas as pl
from jax.experimental.pallas import tpu as pltpu
from jax.sharding import PartitionSpec as P

MINP = 64
NPRE = 7
PBLK = 16
QBLK = 64
LANES = 128
OWN = 5

EPS = 1e-06
INV_TEMP = 20.0
MESH = pl.DeviceIdType.MESH
F32 = jnp.float32
BF16 = jnp.bfloat16


def request_plan(flat_ids, capacity, per_owner):
    entry_count = flat_ids.shape[0]
    is_valid = flat_ids >= 0
    entry_order = jnp.arange(entry_count, dtype=jnp.int32)
    earlier = entry_order[None, :] < entry_order[:, None]
    same_block = (flat_ids[:, None] == flat_ids[None, :]) & is_valid[None, :]
    is_first = is_valid & jnp.logical_not(jnp.any(same_block & earlier, axis=1))
    owner_index = jnp.where(is_valid, flat_ids // per_owner, 0)
    local_block = jnp.where(is_valid, flat_ids % per_owner, 0)
    owner_rank = jnp.sum(
        ((owner_index[:, None] == owner_index[None, :]) & earlier & is_first[None, :]).astype(
            jnp.int32
        ),
        axis=1,
    )
    home_slot = jnp.where(is_first, owner_index * capacity + owner_rank, 0)
    entry_slot = jnp.sum(jnp.where(same_block & is_first[None, :], home_slot[None, :], 0), axis=1)
    return (is_first, home_slot, entry_slot, local_block)


def dot_nt(left, right):
    return lax.dot_general(left, right, (((1,), (1,)), ((), ())), preferred_element_type=F32)


def dot_tn(left, right):
    return lax.dot_general(left, right, (((0,), (0,)), ((), ())), preferred_element_type=F32)


def to_row(column):
    return column.T[0:1, :]


def to_column(row):
    return jnp.broadcast_to(row, (LANES, LANES)).T


def kernel(
    peers, cap, blocks, neg, local_blocks,
    tab, pos_ref, q_ref, p_ref, dq_ref, dp_ref, loss_ref,
    panels, sendbuf, gradbuf, returned, dots, psq, cid, gathered, got, coef, terms, half,
    grid, cols, qsq, rows, small, got_small, back, got_back,
    send1, recv1, send2, recv2, dg_send, dg_recv, sm_send, sm_recv, cf_send, cf_recv,
    sb_send, sb_recv,
):
    me, shard = lax.axis_index("dp"), lax.axis_index("tensor")
    width = q_ref.shape[1]
    chunk = cap * PBLK
    slots = peers * cap
    pairs = blocks // 2
    cand = neg * PBLK
    tiles = slots * PBLK // LANES
    want_at = 0
    slot_at = want_at + slots
    id_at = slot_at + blocks * neg
    ent_at = id_at + blocks * neg
    inv_at = ent_at + blocks * slots
    last = OWN - 1

    barrier = pltpu.get_barrier_semaphore()

    def greet(step, carry):
        pl.semaphore_signal(
            barrier, inc=1, device_id={"dp": lax.rem(me + step, peers)}, device_id_type=MESH
        )
        return carry

    lax.fori_loop(1, peers, greet, 0)
    for step in range(1, 4):
        pl.semaphore_signal(
            barrier, inc=1, device_id={"tensor": lax.rem(shard + step, 4)}, device_id_type=MESH
        )

    def pack(peer, target, offset):
        for k in range(cap):
            block = tab[want_at + peer * cap + k]
            target[pl.ds(offset + k * PBLK, PBLK), :] = p_ref[pl.ds(block * PBLK, PBLK), :]

    def chunk_rows(peer):
        return pl.ds(pl.multiple_of(peer * chunk, PBLK), chunk)

    def fetch(peer):
        return pltpu.make_async_remote_copy(
            src_ref=sendbuf.at[chunk_rows(peer)],
            dst_ref=panels.at[chunk_rows(me)],
            send_sem=send1.at[peer],
            recv_sem=recv1.at[me],
            device_id={"dp": peer},
            device_id_type=MESH,
        )

    def fetched(peer):
        return pltpu.make_async_remote_copy(
            src_ref=sendbuf.at[chunk_rows(me)],
            dst_ref=panels.at[chunk_rows(peer)],
            send_sem=send1.at[me],
            recv_sem=recv1.at[peer],
            device_id={"dp": peer},
            device_id_type=MESH,
        )

    pl.semaphore_wait(barrier, peers - 1 + 3)

    def start_fetch(step, carry):
        peer = lax.rem(me + step, peers)
        pack(peer, sendbuf, pl.multiple_of(peer * chunk, PBLK))
        fetch(peer).start()
        return carry

    lax.fori_loop(1, peers, start_fetch, 0)
    pack(me, panels, pl.multiple_of(me * chunk, PBLK))

    low_half = lax.broadcasted_iota(jnp.int32, (PBLK, LANES), 1) < QBLK
    low_row = lax.broadcasted_iota(jnp.int32, (1, LANES), 1) < QBLK

    def query_terms(j, carry):
        block = q_ref[pl.ds(pl.multiple_of(j * LANES, LANES), LANES), :].astype(F32)
        square = block * block

        def put(k, value):
            qsq[k, pl.ds(j, 1), :] = to_row(jnp.broadcast_to(value, (LANES, LANES)))

        prefix_squares(square, put)
        for e in range(neg):
            low = tab[id_at + (2 * j) * neg + e]
            high = tab[id_at + (2 * j + 1) * neg + e]
            cid[j, e * PBLK : (e + 1) * PBLK, :] = jnp.where(
                low_half, low, high
            ) * PBLK + lax.broadcasted_iota(jnp.int32, (PBLK, LANES), 0)
        return carry

    def prefix_squares(square, put):
        @pl.when(shard == 0)
        def _():
            first = square[:, :LANES]
            total = jnp.sum(jnp.where(low_row, first, 0.0), axis=1, keepdims=True)
            put(0, total)
            total = jnp.sum(first, axis=1, keepdims=True)
            put(1, total)
            for k in range(2, OWN):
                total = total + jnp.sum(
                    square[:, MINP * 2 ** (k - 1) : MINP * 2**k], axis=1, keepdims=True
                )
                put(k, total)

        @pl.when(shard != 0)
        def _():
            put(last, jnp.sum(square, axis=1, keepdims=True))

    lax.fori_loop(0, pairs, query_terms, 0)

    for k in range(OWN):
        half[k, :, cand : cand + PBLK, :] = jnp.zeros((pairs, PBLK, LANES), BF16)
        terms[k, :, cand : cand + PBLK, :] = jnp.zeros((pairs, PBLK, LANES), F32)
    back[...] = jnp.zeros_like(back)
    small[...] = jnp.zeros_like(small)

    def forward(step, carry):
        peer = lax.rem(me + step, peers)

        @pl.when(step > 0)
        def _():
            fetched(peer).wait_recv()

        here = chunk_rows(peer)
        square = panels[here, :].astype(F32)
        square = square * square

        def put(k, value):
            psq[k, here, :] = jnp.broadcast_to(value, (chunk, LANES))

        prefix_squares(square, put)

        def keep(k, value):
            for j in range(pairs):
                dots[k, j, here, :] = value[:, j * LANES : (j + 1) * LANES]

        @pl.when(shard == 0)
        def _():
            first, query = panels[here, :LANES], q_ref[:, :LANES]
            keep(0, dot_nt(jnp.where(low_row, first, jnp.zeros((), BF16)), query))
            total = dot_nt(first, query)
            keep(1, total)
            for k in range(2, OWN):
                span = slice(MINP * 2 ** (k - 1), MINP * 2**k)
                total = total + dot_nt(panels[here, span], q_ref[:, span])
                keep(k, total)

        @pl.when(shard != 0)
        def _():
            keep(last, dot_nt(panels[here, :], q_ref[...]))

        return carry

    lax.fori_loop(0, peers, forward, 0)

    def pick(ref, k, j, lead):
        parts = []
        for e in range(neg):
            low = tab[slot_at + (2 * j) * neg + e] * PBLK
            high = tab[slot_at + (2 * j + 1) * neg + e] * PBLK
            low = ref[lead(k, j) + (pl.ds(low, PBLK),)]
            high = ref[lead(k, j) + (pl.ds(high, PBLK),)]
            parts.append(jnp.where(low_half, low, high))
        return jnp.concatenate(parts, axis=0)

    def pick_dots(k, j):
        return pick(dots, k, j, lambda k, j: (k, j))

    def pick_squares(k, j):
        return pick(psq, k, j, lambda k, j: (k,))

    def small_copy(target, slot):
        return pltpu.make_async_remote_copy(
            src_ref=small, dst_ref=got_small.at[slot], send_sem=sm_send.at[0],
            recv_sem=sm_recv.at[slot], device_id={"tensor": target}, device_id_type=MESH,
        )

    def dots_copy(target, slot, j):
        return pltpu.make_async_remote_copy(
            src_ref=gathered.at[j], dst_ref=got.at[slot, j], send_sem=dg_send.at[j],
            recv_sem=dg_recv.at[slot, j], device_id={"tensor": target}, device_id_type=MESH,
        )

    def later_copy(j):
        return pltpu.make_async_remote_copy(
            src_ref=coef.at[last, j], dst_ref=got.at[0, j], send_sem=cf_send.at[0, j],
            recv_sem=dg_recv.at[0, j], device_id={"tensor": 0}, device_id_type=MESH,
        )

    def half_copy(target, j):
        return pltpu.make_async_remote_copy(
            src_ref=half.at[last, j, pl.ds(0, cand)], dst_ref=half.at[last, j, pl.ds(0, cand)],
            send_sem=cf_send.at[target - 1, j], recv_sem=cf_recv.at[j],
            device_id={"tensor": target}, device_id_type=MESH,
        )

    for t in range(tiles):
        small[t : t + 1, :] = to_row(psq[last, t * LANES : (t + 1) * LANES, :])
    small[tiles : tiles + pairs, :] = qsq[last, 0:pairs, :]

    def widen():
        for t in range(tiles):
            psq[last, t * LANES : (t + 1) * LANES, :] = to_column(small[t : t + 1, :])
        qsq[last, 0:pairs, :] = small[tiles : tiles + pairs, :]

    def each_pair(body):
        def step(j, carry):
            body(j)
            return carry

        lax.fori_loop(0, pairs, step, 0)

    def prefix_terms(products, squares, k, j, weight):
        number = cid[j]
        live = number >= 0
        query_scale = lax.rsqrt(qsq[k, pl.ds(j, 1), :] + EPS)
        passage_scale = jnp.where(live, lax.rsqrt(squares + EPS), 0.0)
        scale = query_scale * passage_scale * INV_TEMP
        logits = products * scale
        exponent = jnp.where(live, jnp.exp(logits), 0.0)
        total = jnp.sum(exponent, axis=0, keepdims=True)
        hit = number == pos_ref[pl.ds(j, 1), :]
        loss = jnp.log(total) - jnp.sum(jnp.where(hit, logits, 0.0), axis=0, keepdims=True)
        gradient = weight * (exponent * (1.0 / total) - jnp.where(hit, 1.0, 0.0))
        inner = gradient * logits
        row = query_scale * query_scale * jnp.sum(inner, axis=0, keepdims=True)
        return gradient * scale, row, passage_scale * passage_scale * inner, weight * loss

    def one_prefix(products, j, weight):
        value, row, column, loss = prefix_terms(
            products, pick_squares(last, j), last, j, weight
        )
        coef[last, j] = value
        terms[last, j, 0:cand, :] = column
        rows[last, pl.ds(j, 1), :] = row
        back[pl.ds(tiles + pairs + j, 1), :] = loss

    def pick_half(ref, k, j, slot):
        low = tab[ent_at + (2 * j) * slots + slot] * PBLK
        high = tab[ent_at + (2 * j + 1) * slots + slot] * PBLK
        return jnp.where(
            low_half,
            ref[k, j, pl.ds(low, PBLK), :],
            ref[k, j, pl.ds(high, PBLK), :],
        )

    def column_sums(count):
        def step(slot, carry):
            for k in range(OWN - count, OWN):
                total = pick_half(terms, k, 0, slot)
                for j in range(1, pairs):
                    total = total + pick_half(terms, k, j, slot)
                cols[k, pl.ds(pl.multiple_of(slot * PBLK, PBLK), PBLK), :] = jnp.broadcast_to(
                    jnp.sum(total, axis=1, keepdims=True), (PBLK, LANES)
                )
            return carry

        lax.fori_loop(0, slots, step, 0)
        for t in range(tiles):
            back[t : t + 1, :] = to_row(cols[last, t * LANES : (t + 1) * LANES, :])
        back[tiles : tiles + pairs, :] = rows[last, 0:pairs, :]

    def back_copy(step, slot):
        return pltpu.make_async_remote_copy(
            src_ref=back, dst_ref=got_back.at[slot], send_sem=sb_send.at[step],
            recv_sem=sb_recv.at[slot], device_id={"tensor": lax.rem(shard + step, 4)},
            device_id_type=MESH,
        )

    def send_back():
        for step in range(1, 4):
            back_copy(step, shard).start()

    @pl.when(shard == 0)
    def _():
        small_copy(1, 0).start()

        def hand_on(j):
            gathered[j] = pick_dots(last, j)
            dots_copy(1, 0, j).start()

        each_pair(hand_on)

        def own(j):
            value = row = column = loss = None
            for k in reversed(range(OWN)):
                products = gathered[j] if k == last else pick_dots(k, j)
                part = prefix_terms(products, pick_squares(k, j), k, j, float(2**k))
                if k == last:
                    value, row, column, loss = part
                else:
                    value, row, column, loss = (
                        value + part[0], row + part[1], column + part[2], loss + part[3]
                    )
                coef[k, j] = value
                rows[k, pl.ds(j, 1), :] = row
                terms[k, j, 0:cand, :] = column
            back[pl.ds(tiles + pairs + j, 1), :] = loss

        each_pair(own)
        column_sums(OWN)
        send_back()

        def finish(j):
            later_copy(j).wait_recv()
            for k in range(OWN):
                half[k, j, 0:cand, :] = (coef[k, j] + got[0, j]).astype(BF16)

        each_pair(finish)
        small_copy(1, 0).wait_send()
        each_pair(lambda j: dots_copy(1, 0, j).wait_send())

    @pl.when(shard == 1)
    def _():
        small_copy(3, 0).wait_recv()
        small[...] = small[...] + got_small[0]
        small_copy(3, 0).start()

        def hand_on(j):
            dots_copy(3, 0, j).wait_recv()
            gathered[j] = pick_dots(last, j) + got[0, j]
            dots_copy(3, 0, j).start()

        each_pair(hand_on)
        widen()
        each_pair(lambda j: one_prefix(gathered[j], j, 32.0))
        column_sums(1)
        send_back()

        def finish(j):
            half_copy(1, j).wait_recv()
            total = coef[last, j] + half[last, j, 0:cand, :].astype(F32)
            coef[last, j] = total
            later_copy(j).start()
            half[last, j, 0:cand, :] = total.astype(BF16)

        each_pair(finish)
        small_copy(3, 0).wait_send()
        each_pair(lambda j: dots_copy(3, 0, j).wait_send())
        each_pair(lambda j: later_copy(j).wait_send())

    @pl.when(shard == 2)
    def _():
        small_copy(3, 1).start()

        def hand_on(j):
            gathered[j] = pick_dots(last, j)
            dots_copy(3, 1, j).start()

        each_pair(hand_on)
        cols[last] = jnp.zeros_like(cols[last])
        rows[last] = jnp.zeros_like(rows[last])
        send_back()
        each_pair(lambda j: half_copy(2, j).wait_recv())
        small_copy(3, 1).wait_send()
        each_pair(lambda j: dots_copy(3, 1, j).wait_send())

    @pl.when(shard == 3)
    def _():
        small_copy(2, 0).wait_recv()
        small_copy(2, 1).wait_recv()
        small[...] = small[...] + got_small[0] + got_small[1]
        widen()

        def answer(j):
            mine = pick_dots(last, j)
            dots_copy(2, 1, j).wait_recv()
            dots_copy(2, 0, j).wait_recv()
            one_prefix(mine + got[0, j] + got[1, j], j, 64.0)
            half[last, j, 0:cand, :] = coef[last, j].astype(BF16)
            half_copy(1, j).start()
            half_copy(2, j).start()

        each_pair(answer)
        column_sums(1)
        send_back()
        each_pair(lambda j: half_copy(1, j).wait_send())
        each_pair(lambda j: half_copy(2, j).wait_send())

    later = jnp.zeros(back.shape, F32)
    loss = back[tiles + pairs : tiles + 2 * pairs, :]
    for step in range(1, 4):
        other = lax.rem(shard + step, 4)
        back_copy(step, other).wait_recv()
        part = got_back[other]
        later = later + jnp.where(other > shard, 1.0, 0.0) * part
        loss = loss + part[tiles + pairs : tiles + 2 * pairs, :]
    weight_total = sum(2.0**k for k in range(NPRE))
    loss_ref[...] = loss / weight_total

    def add_later(count):
        for t in range(tiles):
            extra = to_column(later[t : t + 1, :])
            for k in range(OWN - count, OWN):
                cols[k, t * LANES : (t + 1) * LANES, :] += extra
        for k in range(OWN - count, OWN):
            rows[k, 0:pairs, :] += later[tiles : tiles + pairs, :]

    @pl.when(shard == 0)
    def _():
        add_later(OWN)

    @pl.when(shard != 0)
    def _():
        add_later(1)

    spans = [(k, slice(MINP * 2 ** (k - 1), MINP * 2**k)) for k in range(2, OWN)]

    def build(k, peer):
        def step(i, carry):
            slot = peer * cap + i
            for j in range(pairs):
                grid[
                    k, pl.ds(pl.multiple_of(slot * PBLK, PBLK), PBLK), j * LANES : (j + 1) * LANES
                ] = pick_half(half, k, j, slot)
            return carry

        lax.fori_loop(0, cap, step, 0)

    def send_grad(peer):
        return pltpu.make_async_remote_copy(
            src_ref=gradbuf.at[chunk_rows(peer)], dst_ref=returned.at[me, pl.ds(0, chunk)],
            send_sem=send2.at[peer], recv_sem=recv2.at[me],
            device_id={"dp": peer}, device_id_type=MESH,
        )

    def came_back(peer):
        return pltpu.make_async_remote_copy(
            src_ref=gradbuf.at[chunk_rows(me)], dst_ref=returned.at[peer, pl.ds(0, chunk)],
            send_sem=send2.at[me], recv_sem=recv2.at[peer],
            device_id={"dp": peer}, device_id_type=MESH,
        )

    def passage_part(step, carry):
        peer = lax.rem(me + step, peers)
        here = chunk_rows(peer)

        def put(span, k, product):
            piece = product - cols[k, here, 0:1] * panels[here, span].astype(F32)
            gradbuf[here, span] = piece.astype(BF16)

        @pl.when(shard == 0)
        def _():
            for k in range(OWN):
                build(k, peer)
            query = q_ref[:, :LANES]
            first = panels[here, :LANES].astype(F32)
            low = jnp.dot(grid[0, here, :], query, preferred_element_type=F32)
            low = low - cols[0, here, :] * first
            high = jnp.dot(grid[1, here, :], query, preferred_element_type=F32)
            high = high - cols[1, here, :] * first
            gradbuf[here, :LANES] = jnp.where(low_row, low, high).astype(BF16)
            for k, span in spans:
                put(span, k, jnp.dot(grid[k, here, :], q_ref[:, span], preferred_element_type=F32))

        @pl.when(shard != 0)
        def _():
            build(last, peer)
            put(
                slice(0, width), last,
                jnp.dot(grid[last, here, :], q_ref[...], preferred_element_type=F32),
            )

        @pl.when(step < peers)
        def _():
            send_grad(peer).start()

        @pl.when(step == peers)
        def _():
            returned[me, 0:chunk, :] = gradbuf[here, :]

        return carry

    lax.fori_loop(1, peers + 1, passage_part, 0)

    def query_part(j, carry):
        here = pl.ds(pl.multiple_of(j * LANES, LANES), LANES)

        def column(k):
            return to_column(rows[k, pl.ds(j, 1), :])

        def product(k, span):
            return dot_tn(grid[k, :, here], panels[:, span])

        @pl.when(shard == 0)
        def _():
            query = q_ref[here, :LANES].astype(F32)
            first = slice(0, LANES)
            low = product(0, first) - column(0) * query
            high = product(1, first) - column(1) * query
            dq_ref[here, :LANES] = jnp.where(low_row, low, high).astype(BF16)
            for k, span in spans:
                piece = product(k, span) - column(k)[:, 0:1] * q_ref[here, span].astype(F32)
                dq_ref[here, span] = piece.astype(BF16)

        @pl.when(shard != 0)
        def _():
            piece = product(last, slice(0, width)) - column(last)[:, 0:1] * q_ref[here, :].astype(F32)
            dq_ref[here, :] = piece.astype(BF16)

        return carry

    lax.fori_loop(0, pairs, query_part, 0)

    returned[:, chunk : chunk + PBLK, :] = jnp.zeros((peers, PBLK, width), BF16)

    def drain(step, carry):
        peer = lax.rem(me + step, peers)
        came_back(peer).wait_recv()
        return carry

    lax.fori_loop(1, peers, drain, 0)

    def total_block(block, carry):
        def add(peer, total):
            row = tab[inv_at + peer * local_blocks + block] * PBLK
            return total + returned[peer, pl.ds(row, PBLK), :].astype(F32)

        total = lax.fori_loop(0, peers, add, jnp.zeros((PBLK, width), F32))
        dp_ref[pl.ds(pl.multiple_of(block * PBLK, PBLK), PBLK), :] = total.astype(BF16)
        return carry

    lax.fori_loop(0, local_blocks, total_block, 0)

    def sent(step, carry):
        peer = lax.rem(me + step, peers)
        fetch(peer).wait_send()
        send_grad(peer).wait_send()
        return carry

    lax.fori_loop(1, peers, sent, 0)
    for step in range(1, 4):
        back_copy(step, shard).wait_send()


def per_device(queries, passages, neg_lists, positives):
    peer_count = lax.axis_size("dp")
    width = queries.shape[1]
    blocks_here = neg_lists.shape[0] // peer_count
    neg_count = neg_lists.shape[1]
    local_blocks = passages.shape[0] // PBLK
    capacity = blocks_here * neg_count // 2 // peer_count
    slot_count = peer_count * capacity
    cand = neg_count * PBLK
    pairs = blocks_here // 2
    my_index = lax.axis_index("dp")
    flat_all = neg_lists.reshape(peer_count, blocks_here * neg_count)
    is_first, home_slot, entry_slot, local_block = jax.vmap(
        partial(request_plan, capacity=capacity, per_owner=local_blocks)
    )(flat_all)
    targets = my_index * capacity + jnp.arange(capacity, dtype=jnp.int32)
    target_hit = is_first[:, :, None] & (home_slot[:, :, None] == targets[None, None, :])
    wanted = jnp.sum(jnp.where(target_hit, local_block[:, :, None] + 1, 0), axis=1) - 1
    own_ids = lax.dynamic_index_in_dim(flat_all, my_index, 0, keepdims=False)
    own_slot = lax.dynamic_index_in_dim(entry_slot, my_index, 0, keepdims=False)
    own_live = own_ids >= 0
    entries = jnp.arange(neg_count, dtype=jnp.int32)[None, :, None]
    at_slot = (
        own_slot.reshape(blocks_here, neg_count, 1) == jnp.arange(slot_count, dtype=jnp.int32)
    ) & own_live.reshape(blocks_here, neg_count, 1)
    entry_of = neg_count + jnp.sum(jnp.where(at_slot, entries - neg_count, 0), axis=1)
    named = wanted[:, :, None] == jnp.arange(local_blocks, dtype=jnp.int32)
    ranks = jnp.arange(capacity, dtype=jnp.int32)[None, :, None]
    rank_of = capacity + jnp.sum(jnp.where(named, ranks - capacity, 0), axis=1)
    table = jnp.concatenate([
        jnp.maximum(wanted, 0).reshape(-1),
        jnp.where(own_live, own_slot, 0),
        jnp.where(own_live, own_ids, -1),
        entry_of.reshape(-1),
        rank_of.reshape(-1),
    ]).astype(jnp.int32)

    slot_rows = slot_count * PBLK
    query_count = queries.shape[0]
    smalls = slot_rows // LANES + 2 * pairs
    vmem, dma = pltpu.VMEM, pltpu.SemaphoreType.DMA
    whole = pl.BlockSpec(memory_space=pltpu.VMEM)
    query_grad, passage_grad, loss = pl.pallas_call(
        partial(kernel, peer_count, capacity, blocks_here, neg_count, local_blocks),
        out_shape=(
            jax.ShapeDtypeStruct(queries.shape, BF16),
            jax.ShapeDtypeStruct(passages.shape, BF16),
            jax.ShapeDtypeStruct((pairs, LANES), F32),
        ),
        in_specs=[pl.BlockSpec(memory_space=pltpu.SMEM), whole, whole, whole],
        out_specs=(whole, whole, whole),
        scratch_shapes=[
            vmem((slot_rows, width), BF16),
            vmem((slot_rows, width), BF16),
            vmem((slot_rows, width), BF16),
            vmem((peer_count, (capacity + 1) * PBLK, width), BF16),
            vmem((OWN, pairs, slot_rows, LANES), F32),
            vmem((OWN, slot_rows, LANES), F32),
            vmem((pairs, cand, LANES), jnp.int32),
            vmem((pairs, cand, LANES), F32),
            vmem((2, pairs, cand, LANES), F32),
            vmem((OWN, pairs, cand, LANES), F32),
            vmem((OWN, pairs, cand + PBLK, LANES), F32),
            vmem((OWN, pairs, cand + PBLK, LANES), BF16),
            vmem((OWN, slot_rows, query_count), BF16),
            vmem((OWN, slot_rows, LANES), F32),
            vmem((OWN, 8, LANES), F32),
            vmem((OWN, 8, LANES), F32),
            vmem((smalls, LANES), F32),
            vmem((2, smalls, LANES), F32),
            vmem((smalls, LANES), F32),
            vmem((4, smalls, LANES), F32),
            dma((peer_count,)), dma((peer_count,)), dma((peer_count,)), dma((peer_count,)),
            dma((pairs,)), dma((2, pairs)), dma((1,)), dma((2,)),
            dma((2, pairs)), dma((pairs,)), dma((4,)), dma((4,)),
        ],
        compiler_params=pltpu.CompilerParams(
            collective_id=0, has_side_effects=True, vmem_limit_bytes=56 * 2**20
        ),
        name="matryoshka",
    )(table, positives.reshape(pairs, LANES), queries, passages)
    return query_grad, passage_grad, loss.reshape(query_count)


def solution(mesh):
    return jax.shard_map(
        per_device,
        mesh=mesh,
        in_specs=(P("dp", "tensor"), P("dp", "tensor"), P(), P("dp")),
        out_specs=(P("dp", "tensor"), P("dp", "tensor"), P("dp")),
        check_vma=False,
    )
```

time: 329 us -> 135 us (0.41)
  the two profiles are of different devices: /device:TPU:0 before, /device:TPU:28 now
where the time goes in v1:
time: 135 us
  Pallas kernels  127 us (94%)
  local copies, waits for them, and re-layouts  5.63 us (4%)
  other arithmetic  1.73 us (1%)
    pallas_call x1, Pallas kernels, per_device(): pl.pallas_call(partial(kernel, peer_count, capacity, blocks_here, neg_cou...  127 us
    unnamed x10, local copies, waits for them, and re-layouts  4.45 us

profile of v1, /device:TPU:28, one launch (start us, length us, event | category | flops | bytes accessed | tf_op | source)
XLA Modules:
  0.0 134.7 jit_solution(13995466435333483165)
XLA Ops:
  0.7 0.0 copy-start.1
  0.7 0.7 copy-done.1
  1.4 0.1 copy.8
  1.4 0.1 reshape.216
  1.6 0.1 ge.55
  1.7 0.4 and_reduce_fusion
  2.1 0.4 convert_reduce_fusion
  2.5 0.3 select_reduce_fusion.3
  2.7 0.4 select_reduce_fusion
  3.2 0.1 eq.78
  3.2 0.1 select_reduce_fusion.1
  3.4 0.1 add.107
  3.5 0.1 select_reduce_fusion.2
  3.6 0.1 add.110
  3.7 0.1 max.12
  3.7 0.7 concatenate.3.tab
  4.4 126.6 %matryoshka.1 = (bf16[512,1024]{1,0:T(8,128)(2,1)}, bf16[256,1024]{1,0:T(8,128)(2,1)}, f32[4,128]{1,0:T(4,128)}) custom-call(s32[960]{0:T(1024)} %concatenate.3.tab, s32[4,128]{1,0:T(4,128)} %bitcast.7, bf16[512,1024]{1,0:T(8,128)(2,1)} %q_ref.1, bf16[256,1024]{1,0:T(8,128)(2,1)} %p_ref.1), custom_call_target="tpu_custom_call" | custom-call | tf_op jit(solution)/shard_map/matryoshka/pallas_call | solution.py:641
  131.0 0.0 copy-start
  131.0 2.3 %copy.12 = bf16[512,1024]{1,0:T(8,128)(2,1)} copy(bf16[512,1024]{1,0:T(8,128)(2,1)} %get-tuple-element.20) | data formatting | bytes 2097152
  133.3 0.0 copy-done
  133.3 0.0 copy-start.2
  133.3 0.8 copy.13
  134.1 0.0 copy-done.2
  134.1 0.6 copy.14
  (13 shorter events, 0.1 us)
Async XLA Ops:
  0.7 0.7 copy-start.1
  131.0 2.3 %copy-start = (bf16[256,1024]{1,0:T(8,128)(2,1)S(1)}, bf16[256,1024]{1,0:T(8,128)(2,1)}, u32[]{:S(2)}) copy-start(bf16[256,1024]{1,0:T(8,128)(2,1)} %get-tuple-element.21) | copy-start | bytes 1572868
  133.3 0.8 copy-start.2

commit v2 on v1

--- a/solution.py
+++ b/solution.py
@@ -47,6 +47,14 @@
 
 def dot_tn(left, right):
     return lax.dot_general(left, right, (((0,), (0,)), ((), ())), preferred_element_type=F32)
+
+
+def partner(me, step, peers):
+    other, digit = 0, 1
+    while digit < peers:
+        other = other + lax.rem(lax.div(me, digit) + lax.div(step, digit), 2) * digit
+        digit *= 2
+    return other
 
 
 def to_row(column):
@@ -124,7 +132,7 @@
     pl.semaphore_wait(barrier, peers - 1 + 3)
 
     def start_fetch(step, carry):
-        peer = lax.rem(me + step, peers)
+        peer = partner(me, peers - step, peers)
         pack(peer, sendbuf, pl.multiple_of(peer * chunk, PBLK))
         fetch(peer).start()
         return carry
@@ -178,7 +186,7 @@
     small[...] = jnp.zeros_like(small)
 
     def forward(step, carry):
-        peer = lax.rem(me + step, peers)
+        peer = partner(me, lax.rem(peers - step, peers), peers)
 
         @pl.when(step > 0)
         def _():
@@ -212,6 +220,8 @@
         def _():
             keep(last, dot_nt(panels[here, :], q_ref[...]))
 
+        if chunk == LANES:
+            small[pl.ds(peer, 1), :] = to_row(psq[last, here, :])
         return carry
 
     lax.fori_loop(0, peers, forward, 0)
@@ -257,7 +267,7 @@
             device_id={"tensor": target}, device_id_type=MESH,
         )
 
-    for t in range(tiles):
+    for t in range(tiles if chunk != LANES else 0):
         small[t : t + 1, :] = to_row(psq[last, t * LANES : (t + 1) * LANES, :])
     small[tiles : tiles + pairs, :] = qsq[last, 0:pairs, :]
 
@@ -495,7 +505,7 @@
         )
 
     def passage_part(step, carry):
-        peer = lax.rem(me + step, peers)
+        peer = partner(me, peers - step, peers)
         here = chunk_rows(peer)
 
         def put(span, k, product):

time: 135 us -> 127 us (0.941)
  the two profiles are of different devices: /device:TPU:28 before, /device:TPU:0 now
where the time goes in v2:
time: 127 us
  Pallas kernels  119 us (94%)
  local copies, waits for them, and re-layouts  5.63 us (4%)
  other arithmetic  1.73 us (1%)
    pallas_call x1, Pallas kernels, per_device(): pl.pallas_call(partial(kernel, peer_count, capacity, blocks_here, neg_cou...  119 us
    unnamed x10, local copies, waits for them, and re-layouts  4.45 us

profile of v2, /device:TPU:0, one launch (start us, length us, event | category | flops | bytes accessed | tf_op | source)
XLA Modules:
  0.0 126.9 jit_solution(580209478761467826)
XLA Ops:
  0.7 0.0 copy-start.1
  0.7 0.7 copy-done.1
  1.4 0.1 copy.8
  1.4 0.1 reshape.216
  1.6 0.1 ge.55
  1.7 0.4 and_reduce_fusion
  2.1 0.4 convert_reduce_fusion
  2.5 0.3 select_reduce_fusion.3
  2.7 0.4 select_reduce_fusion
  3.2 0.1 eq.78
  3.2 0.1 select_reduce_fusion.1
  3.4 0.1 add.107
  3.5 0.1 select_reduce_fusion.2
  3.6 0.1 add.110
  3.7 0.1 max.12
  3.7 0.7 concatenate.3.tab
  4.4 118.8 %matryoshka.1 = (bf16[512,1024]{1,0:T(8,128)(2,1)}, bf16[256,1024]{1,0:T(8,128)(2,1)}, f32[4,128]{1,0:T(4,128)}) custom-call(s32[960]{0:T(1024)} %concatenate.3.tab, s32[4,128]{1,0:T(4,128)} %bitcast.7, bf16[512,1024]{1,0:T(8,128)(2,1)} %q_ref.1, bf16[256,1024]{1,0:T(8,128)(2,1)} %p_ref.1), custom_call_target="tpu_custom_call" | custom-call | tf_op jit(solution)/shard_map/matryoshka/pallas_call | solution.py:651
  123.2 0.0 copy-start
  123.2 2.3 %copy.12 = bf16[512,1024]{1,0:T(8,128)(2,1)} copy(bf16[512,1024]{1,0:T(8,128)(2,1)} %get-tuple-element.20) | data formatting | bytes 2097152
  125.5 0.0 copy-done
  125.5 0.0 copy-start.2
  125.5 0.8 copy.13
  126.3 0.0 copy-done.2
  126.3 0.6 copy.14
  (13 shorter events, 0.1 us)
Async XLA Ops:
  0.7 0.7 copy-start.1
  123.2 2.3 %copy-start = (bf16[256,1024]{1,0:T(8,128)(2,1)S(1)}, bf16[256,1024]{1,0:T(8,128)(2,1)}, u32[]{:S(2)}) copy-start(bf16[256,1024]{1,0:T(8,128)(2,1)} %get-tuple-element.21) | copy-start | bytes 1572868
  125.5 0.8 copy-start.2

commit v3 on v2

--- a/solution.py
+++ b/solution.py
@@ -68,7 +68,7 @@
 def kernel(
     peers, cap, blocks, neg, local_blocks,
     tab, pos_ref, q_ref, p_ref, dq_ref, dp_ref, loss_ref,
-    panels, sendbuf, gradbuf, returned, dots, psq, cid, gathered, got, coef, terms, half,
+    panels, sendbuf, gradbuf, near, far, total_grad, dots, psq, cid, gathered, got, coef, terms, half,
     grid, cols, qsq, rows, small, got_small, back, got_back,
     send1, recv1, send2, recv2, dg_send, dg_recv, sm_send, sm_recv, cf_send, cf_recv,
     sb_send, sb_recv,
@@ -490,22 +490,22 @@
 
         lax.fori_loop(0, cap, step, 0)
 
-    def send_grad(peer):
+    split = peers // 2
+
+    def landing(step, is_far):
+        return far.at[step - split] if is_far else near.at[step]
+
+    def grad_copy(step, is_far):
+        peer = partner(me, step, peers)
         return pltpu.make_async_remote_copy(
-            src_ref=gradbuf.at[chunk_rows(peer)], dst_ref=returned.at[me, pl.ds(0, chunk)],
-            send_sem=send2.at[peer], recv_sem=recv2.at[me],
+            src_ref=gradbuf.at[chunk_rows(peer)],
+            dst_ref=landing(step, is_far).at[pl.ds(0, chunk)],
+            send_sem=send2.at[step], recv_sem=recv2.at[step],
             device_id={"dp": peer}, device_id_type=MESH,
         )
 
-    def came_back(peer):
-        return pltpu.make_async_remote_copy(
-            src_ref=gradbuf.at[chunk_rows(me)], dst_ref=returned.at[peer, pl.ds(0, chunk)],
-            send_sem=send2.at[me], recv_sem=recv2.at[peer],
-            device_id={"dp": peer}, device_id_type=MESH,
-        )
-
-    def passage_part(step, carry):
-        peer = partner(me, peers - step, peers)
+    def passage_part(step):
+        peer = partner(me, step, peers)
         here = chunk_rows(peer)
 
         def put(span, k, product):
@@ -534,17 +534,20 @@
                 jnp.dot(grid[last, here, :], q_ref[...], preferred_element_type=F32),
             )
 
-        @pl.when(step < peers)
-        def _():
-            send_grad(peer).start()
-
-        @pl.when(step == peers)
-        def _():
-            returned[me, 0:chunk, :] = gradbuf[here, :]
-
-        return carry
-
-    lax.fori_loop(1, peers + 1, passage_part, 0)
+    def far_part(i, carry):
+        passage_part(peers - 1 - i)
+        grad_copy(peers - 1 - i, True).start()
+        return carry
+
+    def near_part(i, carry):
+        passage_part(split - i)
+        grad_copy(split - i, False).start()
+        return carry
+
+    lax.fori_loop(0, split, far_part, 0)
+    lax.fori_loop(1, split, near_part, 0)
+    passage_part(0)
+    near[0, 0:chunk, :] = gradbuf[chunk_rows(me), :]
 
     def query_part(j, carry):
         here = pl.ds(pl.multiple_of(j * LANES, LANES), LANES)
@@ -575,35 +578,72 @@
 
     lax.fori_loop(0, pairs, query_part, 0)
 
-    returned[:, chunk : chunk + PBLK, :] = jnp.zeros((peers, PBLK, width), BF16)
-
-    def drain(step, carry):
-        peer = lax.rem(me + step, peers)
-        came_back(peer).wait_recv()
-        return carry
-
-    lax.fori_loop(1, peers, drain, 0)
-
-    def total_block(block, carry):
-        def add(peer, total):
+    zeros = jnp.zeros((split, PBLK, width), BF16)
+    near[:, chunk : chunk + PBLK, :] = zeros
+    far[:, chunk : chunk + PBLK, :] = zeros
+
+    def add_up(ref, first, block, total):
+        def add(i, total):
+            peer = partner(me, first + i, peers)
             row = tab[inv_at + peer * local_blocks + block] * PBLK
-            return total + returned[peer, pl.ds(row, PBLK), :].astype(F32)
-
-        total = lax.fori_loop(0, peers, add, jnp.zeros((PBLK, width), F32))
-        dp_ref[pl.ds(pl.multiple_of(block * PBLK, PBLK), PBLK), :] = total.astype(BF16)
-        return carry
-
-    lax.fori_loop(0, local_blocks, total_block, 0)
+            return total + ref[i, pl.ds(row, PBLK), :].astype(F32)
+
+        return lax.fori_loop(0, split, add, total)
+
+    def block_rows(block):
+        return pl.ds(pl.multiple_of(block * PBLK, PBLK), PBLK)
+
+    def drain_near(step, carry):
+        grad_copy(step, False).wait_recv()
+        return carry
+
+    def near_block(block, carry):
+        total_grad[block_rows(block), :] = add_up(near, 0, block, jnp.zeros((PBLK, width), F32))
+        return carry
+
+    def drain_far(i, carry):
+        grad_copy(split + i, True).wait_recv()
+        return carry
+
+    def far_block(block, carry):
+        total = add_up(far, split, block, total_grad[block_rows(block), :])
+        dp_ref[block_rows(block), :] = total.astype(BF16)
+        return carry
+
+    lax.fori_loop(1, split, drain_near, 0)
+    lax.fori_loop(0, local_blocks, near_block, 0)
+    lax.fori_loop(0, split, drain_far, 0)
+    lax.fori_loop(0, local_blocks, far_block, 0)
 
     def sent(step, carry):
-        peer = lax.rem(me + step, peers)
-        fetch(peer).wait_send()
-        send_grad(peer).wait_send()
+        fetch(partner(me, step, peers)).wait_send()
+        return carry
+
+    def near_sent(step, carry):
+        grad_copy(step, False).wait_send()
+        return carry
+
+    def far_sent(i, carry):
+        grad_copy(split + i, True).wait_send()
         return carry
 
     lax.fori_loop(1, peers, sent, 0)
+    lax.fori_loop(1, split, near_sent, 0)
+    lax.fori_loop(0, split, far_sent, 0)
     for step in range(1, 4):
         back_copy(step, shard).wait_send()
+
+
+def copy_out(*refs):
+    sources, targets, done = refs[:3], refs[3:6], refs[6]
+    copies = [
+        pltpu.make_async_copy(source, target, done.at[i])
+        for i, (source, target) in enumerate(zip(sources, targets))
+    ]
+    for copy in copies:
+        copy.start()
+    for copy in copies:
+        copy.wait()
 
 
 def per_device(queries, passages, neg_lists, positives):
@@ -661,7 +701,9 @@
             vmem((slot_rows, width), BF16),
             vmem((slot_rows, width), BF16),
             vmem((slot_rows, width), BF16),
-            vmem((peer_count, (capacity + 1) * PBLK, width), BF16),
+            vmem((peer_count // 2, (capacity + 1) * PBLK, width), BF16),
+            vmem((peer_count // 2, (capacity + 1) * PBLK, width), BF16),
+            vmem(passages.shape, F32),
             vmem((OWN, pairs, slot_rows, LANES), F32),
             vmem((OWN, slot_rows, LANES), F32),
             vmem((pairs, cand, LANES), jnp.int32),
@@ -687,6 +729,16 @@
         ),
         name="matryoshka",
     )(table, positives.reshape(pairs, LANES), queries, passages)
+    results = (query_grad, passage_grad, loss)
+    anywhere = pl.BlockSpec(memory_space=pl.ANY)
+    query_grad, passage_grad, loss = pl.pallas_call(
+        copy_out,
+        out_shape=tuple(jax.ShapeDtypeStruct(part.shape, part.dtype) for part in results),
+        in_specs=[anywhere] * 3,
+        out_specs=(anywhere,) * 3,
+        scratch_shapes=[dma((3,))],
+        name="copy_out",
+    )(*results)
     return query_grad, passage_grad, loss.reshape(query_count)
 
 

time: 127 us -> 172 us (1.35)
  Pallas kernels: 119 us -> 168 us
  local copies, waits for them, and re-layouts: 5.63 us -> 1.93 us
    pallas_call x0 -> x1, Pallas kernels: none -> 48.8 us  [per_device(): pl.pallas_call(copy_out, out_shape=tuple((jax.ShapeDtypeStruct(part.shape...]
    unnamed x10 -> x3, local copies, waits for them, and re-layouts: 4.45 us -> 0.75 us
where the time goes in v3:
time: 172 us
  Pallas kernels  168 us (98%)
  local copies, waits for them, and re-layouts  1.93 us (1%)
  other arithmetic  1.73 us (1%)
    pallas_call x1, Pallas kernels, per_device(): pl.pallas_call(partial(kernel, peer_count, capacity, blocks_here, neg_cou...  119 us
    pallas_call x1, Pallas kernels, per_device(): pl.pallas_call(copy_out, out_shape=tuple((jax.ShapeDtypeStruct(part.shape...  48.8 us

profile of v3, /device:TPU:0, one launch (start us, length us, event | category | flops | bytes accessed | tf_op | source)
XLA Modules:
  0.0 172.0 jit_solution(14728476100919730733)
XLA Ops:
  0.7 0.0 copy-start
  0.7 0.7 copy-done
  1.4 0.1 copy.8
  1.4 0.1 reshape.216
  1.6 0.1 ge.55
  1.7 0.4 and_reduce_fusion
  2.1 0.4 convert_reduce_fusion
  2.5 0.3 select_reduce_fusion.3
  2.7 0.4 select_reduce_fusion
  3.2 0.1 eq.78
  3.2 0.1 select_reduce_fusion.1
  3.4 0.1 add.107
  3.5 0.1 select_reduce_fusion.2
  3.6 0.1 add.110
  3.7 0.1 max.12
  3.7 0.7 concatenate.3.tab
  4.4 118.7 %matryoshka.1 = (bf16[512,1024]{1,0:T(8,128)(2,1)}, bf16[256,1024]{1,0:T(8,128)(2,1)}, f32[4,128]{1,0:T(4,128)}) custom-call(s32[960]{0:T(1024)} %concatenate.3.tab, s32[4,128]{1,0:T(4,128)} %bitcast.7, bf16[512,1024]{1,0:T(8,128)(2,1)} %q_ref.1, bf16[256,1024]{1,0:T(8,128)(2,1)} %p_ref.1), custom_call_target="tpu_custom_call" | custom-call | tf_op jit(solution)/shard_map/matryoshka/pallas_call | solution.py:691
  123.1 48.8 %copy_out.1 = (bf16[512,1024]{1,0:T(8,128)(2,1)}, bf16[256,1024]{1,0:T(8,128)(2,1)}, f32[4,128]{1,0:T(4,128)}) custom-call(bf16[512,1024]{1,0:T(8,128)(2,1)} %get-tuple-element.9.refs_0_, bf16[256,1024]{1,0:T(8,128)(2,1)} %get-tuple-element.10.refs_1_, f32[4,128]{1,0:T(4,128)} %get-tuple-element.11.refs_2_), custom_call_target="tpu_custom_call" | custom-call | tf_op jit(solution)/shard_map/copy_out/pallas_call | solution.py:734
  (13 shorter events, 0.1 us)
Async XLA Ops:
  0.7 0.7 copy-start

commit v4 on v3

--- a/solution.py
+++ b/solution.py
@@ -549,34 +549,25 @@
     passage_part(0)
     near[0, 0:chunk, :] = gradbuf[chunk_rows(me), :]
 
-    def query_part(j, carry):
-        here = pl.ds(pl.multiple_of(j * LANES, LANES), LANES)
-
-        def column(k):
-            return to_column(rows[k, pl.ds(j, 1), :])
-
-        def product(k, span):
-            return dot_tn(grid[k, :, here], panels[:, span])
-
-        @pl.when(shard == 0)
-        def _():
-            query = q_ref[here, :LANES].astype(F32)
-            first = slice(0, LANES)
-            low = product(0, first) - column(0) * query
-            high = product(1, first) - column(1) * query
-            dq_ref[here, :LANES] = jnp.where(low_row, low, high).astype(BF16)
-            for k, span in spans:
-                piece = product(k, span) - column(k)[:, 0:1] * q_ref[here, span].astype(F32)
-                dq_ref[here, span] = piece.astype(BF16)
-
-        @pl.when(shard != 0)
-        def _():
-            piece = product(last, slice(0, width)) - column(last)[:, 0:1] * q_ref[here, :].astype(F32)
-            dq_ref[here, :] = piece.astype(BF16)
-
-        return carry
-
-    lax.fori_loop(0, pairs, query_part, 0)
+    def query_part(k, span):
+        column = jnp.concatenate(
+            [to_column(rows[k, j : j + 1, :])[:, 0:1] for j in range(pairs)], axis=0
+        )
+        return dot_tn(grid[k], panels[:, span]) - column * q_ref[:, span].astype(F32)
+
+    @pl.when(shard == 0)
+    def _():
+        first = slice(0, LANES)
+        piece = jnp.where(low_row, query_part(0, first), query_part(1, first))
+        dq_ref[:, first] = piece.astype(BF16)
+        for k, span in spans:
+            dq_ref[:, span] = query_part(k, span).astype(BF16)
+
+    @pl.when(shard != 0)
+    def _():
+        for start in range(0, width, 2 * LANES):
+            span = slice(start, start + 2 * LANES)
+            dq_ref[:, span] = query_part(last, span).astype(BF16)
 
     zeros = jnp.zeros((split, PBLK, width), BF16)
     near[:, chunk : chunk + PBLK, :] = zeros
@@ -635,15 +626,25 @@
 
 
 def copy_out(*refs):
-    sources, targets, done = refs[:3], refs[3:6], refs[6]
-    copies = [
-        pltpu.make_async_copy(source, target, done.at[i])
-        for i, (source, target) in enumerate(zip(sources, targets))
-    ]
-    for copy in copies:
-        copy.start()
-    for copy in copies:
-        copy.wait()
+    sources, targets, held, arrived, left = refs[:3], refs[3:6], refs[6:9], refs[9], refs[10]
+    parts, number = [], 0
+    for source, target, hold in zip(sources, targets, held):
+        count = source.shape[0]
+        step = min(count, LANES)
+        for start in range(0, count, step):
+            part = pl.ds(start, step)
+            parts.append((
+                pltpu.make_async_copy(source.at[part], hold.at[part], arrived.at[number]),
+                pltpu.make_async_copy(hold.at[part], target.at[part], left.at[number]),
+            ))
+            number += 1
+    for arrive, leave in parts:
+        arrive.start()
+    for arrive, leave in parts:
+        arrive.wait()
+        leave.start()
+    for arrive, leave in parts:
+        leave.wait()
 
 
 def per_device(queries, passages, neg_lists, positives):
@@ -730,13 +731,15 @@
         name="matryoshka",
     )(table, positives.reshape(pairs, LANES), queries, passages)
     results = (query_grad, passage_grad, loss)
+    pieces = sum(-(-part.shape[0] // LANES) for part in results)
     anywhere = pl.BlockSpec(memory_space=pl.ANY)
     query_grad, passage_grad, loss = pl.pallas_call(
         copy_out,
         out_shape=tuple(jax.ShapeDtypeStruct(part.shape, part.dtype) for part in results),
         in_specs=[anywhere] * 3,
         out_specs=(anywhere,) * 3,
-        scratch_shapes=[dma((3,))],
+        scratch_shapes=[vmem(part.shape, part.dtype) for part in results]
+        + [dma((pieces,)), dma((pieces,))],
         name="copy_out",
     )(*results)
     return query_grad, passage_grad, loss.reshape(query_count)

time: 172 us -> 126 us (0.73)
  Pallas kernels: 168 us -> 121 us
    pallas_call x1, Pallas kernels: 48.8 us -> 2.21 us  [per_device(): pl.pallas_call(copy_out, out_shape=tuple((jax.ShapeDtypeStruct(part.shape...]
where the time goes in v4:
time: 126 us; the launch traced here: 125 us
  Pallas kernels  121 us (96%)
  local copies, waits for them, and re-layouts  1.93 us (2%)
  other arithmetic  1.73 us (1%)
    pallas_call x1, Pallas kernels, per_device(): pl.pallas_call(partial(kernel, peer_count, capacity, blocks_here, neg_cou...  119 us

profile of v4, /device:TPU:0, one launch (start us, length us, event | category | flops | bytes accessed | tf_op | source)
XLA Modules:
  0.0 125.3 jit_solution(2180637351818128641)
XLA Ops:
  0.7 0.0 copy-start
  0.7 0.7 copy-done
  1.4 0.1 copy.8
  1.4 0.1 reshape.216
  1.6 0.1 ge.55
  1.7 0.4 and_reduce_fusion
  2.1 0.4 convert_reduce_fusion
  2.5 0.3 select_reduce_fusion.3
  2.7 0.4 select_reduce_fusion
  3.2 0.1 eq.78
  3.2 0.1 select_reduce_fusion.1
  3.4 0.1 add.107
  3.5 0.1 select_reduce_fusion.2
  3.6 0.1 add.110
  3.7 0.1 max.12
  3.7 0.7 concatenate.3.tab
  4.4 118.7 %matryoshka.1 = (bf16[512,1024]{1,0:T(8,128)(2,1)}, bf16[256,1024]{1,0:T(8,128)(2,1)}, f32[4,128]{1,0:T(4,128)}) custom-call(s32[960]{0:T(1024)} %concatenate.3.tab, s32[4,128]{1,0:T(4,128)} %bitcast.7, bf16[512,1024]{1,0:T(8,128)(2,1)} %q_ref.1, bf16[256,1024]{1,0:T(8,128)(2,1)} %p_ref.1), custom_call_target="tpu_custom_call" | custom-call | tf_op jit(solution)/shard_map/matryoshka/pallas_call | solution.py:692
  123.1 2.2 %copy_out.1 = (bf16[512,1024]{1,0:T(8,128)(2,1)}, bf16[256,1024]{1,0:T(8,128)(2,1)}, f32[4,128]{1,0:T(4,128)}) custom-call(bf16[512,1024]{1,0:T(8,128)(2,1)} %get-tuple-element.9.refs_0_, bf16[256,1024]{1,0:T(8,128)(2,1)} %get-tuple-element.10.refs_1_, f32[4,128]{1,0:T(4,128)} %get-tuple-element.11.refs_2_), custom_call_target="tpu_custom_call" | custom-call | tf_op jit(solution)/shard_map/copy_out/pallas_call | solution.py:736
  (13 shorter events, 0.1 us)
Async XLA Ops:
  0.7 0.7 copy-start
